TPU v7x, 128 devices: a whole 4x4x4 slice. The times are simulated.
128 devices in a mesh: row: 16 (over y, x), col: 8 (over z, core).
Axes of the slice: x: 4, y: 4, z: 4, core: 2. Of those that a mesh axis runs over, the one named last changes fastest.
Arguments:
- out_grad: bfloat16 [131072, 256], P(('row', 'col')), may hold values from -6 to 6
- features: bfloat16 [131072, 256], P(('col', 'row')), may hold values from -6 to 6
- weight: bfloat16 [256, 256], replicated, may hold values from -0.375 to 0.375
- tiles: bfloat16 [16, 8, 384, 128, 128], P('row', 'col'), may hold values from -0.07470703 to 0.07470703
- row_block: int32 [16, 8, 384], P('row', 'col'), may hold values from 0 to 63
- col_block: int32 [16, 8, 384], P('row', 'col'), may hold values from 0 to 127
- live: int32 [16, 8, 384], P('row', 'col'), may hold values from 0 to 1, as said below
Outputs:
- input_grad: bfloat16 [131072, 256], P(('col', 'row'))
- weight_grad: float32 [256, 256], replicated
Inputs may be any that keep to these rules, and one draw needn't show every extreme that they name: Each cell's slots of live hold between 48 and 384 ones, and in some cell all 384 slots are live.
All inputs are finite; a program needn't handle non-finite values.
Results may differ from a plain program's by a relative error of at most 0.0049.
Values may be sent and summed in bfloat16 or wider, within the bound.
No kernel may reach another device: no remote copies, remote signals or barrier semaphores. Data moves between devices by JAX's collectives and lax.ppermute only.
A program may use at most 256 MiB of HBM per device.

v0:
```python
import jax
import jax.numpy as jnp
from jax import lax
from jax.sharding import PartitionSpec as P


def local(out_grad, features, weight, tiles, row_block, col_block, live):
    tile_set = tiles[0, 0]
    row_ids = row_block[0, 0]
    col_ids = col_block[0, 0]
    live_weights = live[0, 0].astype(jnp.float32)
    tile_size = tile_set.shape[-1]
    feature_width = out_grad.shape[1]
    own_rows = features.shape[0]
    group_rows = lax.all_gather(out_grad, "col", axis=0, tiled=True)
    grad_blocks = group_rows.reshape(-1, tile_size, feature_width)
    column_count = lax.axis_size("row") * own_rows // tile_size
    panels = grad_blocks[row_ids]
    contrib = jnp.einsum("kij,kif->kjf", tile_set, panels, preferred_element_type=jnp.float32)
    contrib = contrib * live_weights[:, None, None]
    partial_value = jax.ops.segment_sum(contrib, col_ids, num_segments=column_count)
    partial_value = partial_value.reshape(column_count * tile_size, feature_width)
    summed = lax.psum_scatter(partial_value, "row", scatter_dimension=0, tiled=True)
    column_grad = summed.astype(jnp.bfloat16)
    input_grad = jnp.einsum(
        "nf,gf->ng", column_grad, weight, preferred_element_type=jnp.float32
    ).astype(jnp.bfloat16)
    local_weight = jnp.einsum(
        "nf,ng->fg", features, column_grad, preferred_element_type=jnp.float32
    )
    summed_weight = lax.psum(local_weight, ("row", "col"))
    node_count = own_rows * lax.axis_size("row") * lax.axis_size("col")
    weight_grad = summed_weight * node_count ** (-0.5)
    return (input_grad, weight_grad)


def solution(mesh):
    return jax.shard_map(
        local,
        mesh=mesh,
        in_specs=(
            P(("row", "col"), None),
            P(("col", "row"), None),
            P(),
            P("row", "col", None, None, None),
            P("row", "col", None),
            P("row", "col", None),
            P("row", "col", None),
        ),
        out_specs=(P(("col", "row"), None), P()),
        check_vma=False,
    )
```

profile of v0, /device:TPU:1, one launch (start us, length us, event | category | flops | bytes accessed | tf_op | source)
XLA Modules:
  0.0 529.0 jit_solution(17368533770410654152)
XLA Ops:
  7.2 0.0 copy-start
  7.2 0.0 all-gather.2.cloned.1.call-start
  7.2 0.7 all-gather.2.cloned.1.call-update
  7.9 0.0 reduce-scatter.2.cloned.1.call-start
  8.0 0.7 reduce
  8.7 0.7 fusion.3
  9.4 0.7 convert_reduce_fusion
  10.1 35.7 %all-gather.2.cloned.1.call-done = bf16[8192,256]{1,0:T(8,128)(2,1)} async-done(((bf16[1024,256]{1,0:T(8,128)(2,1)}), bf16[8192,256]{1,0:T(8,128)(2,1)}) %all-gather.2.cloned.1.call-update) | async-done | bytes 4194320 | tf_op jit(solution)/shard_map/all_gather | solution.py:15
  45.7 15.1 %gather_fusion = bf16[384,128,256]{2,1,0:T(8,128)(2,1)} fusion(bf16[64,128,256]{2,1,0:T(8,128)(2,1)} %bitcast.15, s32[1024]{0:T(1024)S(1)} %pad_clamp_fusion), kind=kCustom, calls=%fused_computation | custom fusion | bytes 50333184 | tf_op jit(solution)/shard_map/gather | solution.py:18
  60.9 31.7 %multiply_bitcast_fusion = f32[384,128,256]{1,2,0:T(8,128)} fusion(f32[384]{0:T(512)S(1)} %convert_reduce_fusion, bf16[384,128,256]{2,1,0:T(8,128)(2,1)} %gather_fusion, bf16[1,1,384,128,128]{4,3,2,1,0:T(8,128)(2,1)} %param.10), kind=kOutput, calls=%fused_computation.2 | convolution fusion | flops 3233808384 | bytes 88081920 | tf_op jit(solution)/shard_map/kij,kif->kjf/dot_general | solution.py:19
  92.6 48.8 %copy.12 = f32[384,128,256]{2,1,0:T(8,128)} copy(f32[384,128,256]{1,2,0:T(8,128)} %multiply_bitcast_fusion) | data formatting | bytes 100663296 | tf_op jit(solution)/shard_map/mul | solution.py:20
  141.4 7.8 %broadcast_in_dim.2 = f32[128,128,256]{2,1,0:T(8,128)} broadcast(f32[]{:T(128)} %constant.0.clone.1), dimensions={} | broadcast | bytes 16777220 | tf_op jit(solution)/shard_map/broadcast_in_dim | solution.py:21
  149.2 114.9 %scatter_fusion = f32[128,128,256]{2,1,0:T(8,128)} fusion(f32[128,128,256]{2,1,0:T(8,128)} %broadcast_in_dim.2, s32[384]{0:T(512)S(1)} %reduce, f32[384,128,256]{2,1,0:T(8,128)} %copy.12), kind=kCustom, calls=%fused_computation.1 | custom fusion | flops 12582912 | bytes 150996480 | tf_op jit(solution)/shard_map/scatter-add | solution.py:21
  264.1 0.0 reduce-scatter.2.cloned.1.call-update
  264.1 0.0 all-reduce.2.cloned.1.call-start
  264.1 109.6 %reduce-scatter.2.cloned.1.call-done = f32[1024,256]{1,0:T(8,128)} async-done(((f32[16384,256]{1,0:T(8,128)}), f32[1024,256]{1,0:T(8,128)}) %reduce-scatter.2.cloned.1.call-update) | async-done | bytes 1048592 | tf_op jit(solution)/shard_map/reduce_scatter | solution.py:23
  373.7 0.0 copy-done
  373.8 2.3 convolution_bitcast_fusion
  376.0 0.0 all-reduce.2.cloned.1.call-update
  376.0 0.0 copy-done.1
  376.1 2.4 convolution_convert_fusion
  378.4 142.3 %all-reduce.2.cloned.1.call-done = f32[256,256]{0,1:T(8,128)} async-done(((f32[256,256]{0,1:T(8,128)}), f32[256,256]{0,1:T(8,128)}) %all-reduce.2.cloned.1.call-update) | async-done | bytes 262160 | tf_op jit(solution)/shard_map/psum | solution.py:31
  520.7 1.0 broadcast_multiply_fusion
  521.7 0.8 copy.13
  (2 shorter events, 0.0 us)
Async XLA Ops:
  7.2 366.6 %copy-start = (bf16[1024,256]{1,0:T(8,128)(2,1)S(1)}, bf16[1024,256]{1,0:T(8,128)(2,1)}, u32[]{:S(2)}) copy-start(bf16[1024,256]{1,0:T(8,128)(2,1)} %param.8) | copy-start | bytes 1572868
  7.2 38.5 %all-gather.2.cloned.1.call-start = ((), (), s32[]{:S(2)}) async-start(), calls=%async_computation.1 | async-start | bytes 4718592 | tf_op jit(solution)/shard_map/all_gather | solution.py:15
  7.9 365.8 %reduce-scatter.2.cloned.1.call-start = ((), (), s32[]{:S(2)}) async-start(), calls=%async_computation.2 | async-start | bytes 17825792 | tf_op jit(solution)/shard_map/reduce_scatter | solution.py:23
  149.2 226.9 %copy-start.1 = (bf16[256,256]{1,0:T(8,128)(2,1)S(1)}, bf16[256,256]{1,0:T(8,128)(2,1)}, u32[]{:S(2)}) copy-start(bf16[256,256]{1,0:T(8,128)(2,1)} %param.9) | copy-start | bytes 393220
  264.1 256.6 %all-reduce.2.cloned.1.call-start = ((), (), s32[]{:S(2)}) async-start(), calls=%async_computation.3 | async-start | bytes 524288 | tf_op jit(solution)/shard_map/psum | solution.py:31
Sparse Core Ops, SparseCore 0:
  9.7 35.9 all-gather.1
  264.2 109.5 reduce-scatter.1
  379.1 141.5 all-reduce.1
where the time goes:
time: 530 us; the launch traced here: 529 us
  waiting for transfers between devices  288 us (54%)
  other arithmetic  118 us (22%)
  local copies, waits for them, and re-layouts  72.6 us (14%)
  matrix products  36.3 us (7%)
  between operations  13.8 us (3%)
    psum x1, waiting for transfers between devices, local(): summed_weight = lax.psum(local_weight, ('row', 'col'))  142 us
    scatter-add x1, other arithmetic, local(): jax.ops.segment_sum(contrib, col_ids, num_segments=column_count)  115 us
    reduce_scatter x1, waiting for transfers between devices, local(): lax.psum_scatter(partial_value, 'row', scatter_dimension=0, tiled=True)  110 us
    mul x1, local copies, waits for them, and re-layouts, local(): contrib = contrib * live_weights[:, None, None]  48.8 us
    all_gather x1, waiting for transfers between devices, local(): group_rows = lax.all_gather(out_grad, 'col', axis=0, tiled=True)  35.7 us
    dot_general x1, matrix products, local(): jnp.einsum('kij,kif->kjf', tile_set, panels, preferred_element_type=jnp.f...  31.7 us
    gather x1, local copies, waits for them, and re-layouts, local(): panels = grad_blocks[row_ids]  15.1 us
  transfers between devices with their start and end apart: 3, of which 3 were waited for; matrix products, arithmetic and copies ran while one was open for 1% of the time, Pallas kernels for 0%

commit v1 on v0

--- a/solution.py
+++ b/solution.py
@@ -12,7 +12,9 @@
     tile_size = tile_set.shape[-1]
     feature_width = out_grad.shape[1]
     own_rows = features.shape[0]
-    group_rows = lax.all_gather(out_grad, "col", axis=0, tiled=True)
+    group_rows = jnp.concatenate(
+        lax.all_to_all(jnp.stack([out_grad] * lax.axis_size("col")), "col", 0, 0), axis=0
+    )
     grad_blocks = group_rows.reshape(-1, tile_size, feature_width)
     column_count = lax.axis_size("row") * own_rows // tile_size
     panels = grad_blocks[row_ids]

time: 530 us -> 552 us (1.042)
  waiting for transfers between devices: 288 us -> 299 us
  starting transfers between devices: 0.12 us -> 6.86 us
    all_to_all x0 -> x1, waiting for transfers between devices: none -> 46.8 us  [local(): lax.all_to_all(jnp.stack([out_grad] * lax.axis_size('col')), 'col', 0, 0)]
    all_gather x1 -> x0, waiting for transfers between devices: 35.7 us -> none  [local(): group_rows = lax.all_gather(out_grad, 'col', axis=0, tiled=True)]
    all_to_all x0 -> x1, starting transfers between devices: none -> 6.81 us  [local(): lax.all_to_all(jnp.stack([out_grad] * lax.axis_size('col')), 'col', 0, 0)]
where the time goes in v1:
time: 552 us; the launch traced here: 551 us
  waiting for transfers between devices  299 us (54%)
  other arithmetic  118 us (21%)
  local copies, waits for them, and re-layouts  75.9 us (14%)
  matrix products  36.4 us (7%)
  between operations  14.1 us (3%)
  starting transfers between devices  6.86 us (1%)
    psum x1, waiting for transfers between devices, local(): summed_weight = lax.psum(local_weight, ('row', 'col'))  142 us
    scatter-add x1, other arithmetic, local(): jax.ops.segment_sum(contrib, col_ids, num_segments=column_count)  115 us
    reduce_scatter x1, waiting for transfers between devices, local(): lax.psum_scatter(partial_value, 'row', scatter_dimension=0, tiled=True)  110 us
    mul x1, local copies, waits for them, and re-layouts, local(): contrib = contrib * live_weights[:, None, None]  48.8 us
    all_to_all x1, waiting for transfers between devices, local(): lax.all_to_all(jnp.stack([out_grad] * lax.axis_size('col')), 'col', 0, 0)  46.8 us
    dot_general x1, matrix products, local(): jnp.einsum('kij,kif->kjf', tile_set, panels, preferred_element_type=jnp.f...  31.7 us
    gather x1, local copies, waits for them, and re-layouts, local(): panels = grad_blocks[row_ids]  15.1 us
  transfers between devices with their start and end apart: 3, of which 3 were waited for; matrix products, arithmetic and copies ran while one was open for 1% of the time, Pallas kernels for 0%

profile of v1, /device:TPU:1, one launch (start us, length us, event | category | flops | bytes accessed | tf_op | source)
XLA Modules:
  0.0 550.5 jit_solution(7422897808771373747)
XLA Ops:
  7.2 0.0 copy-start
  7.2 3.3 stack.2
  10.5 6.8 %all-to-all-start = ((bf16[8,1024,256]{2,1,0:T(8,128)(2,1)}), bf16[8,1024,256]{2,1,0:T(8,128)(2,1)}, u32[]{:S(2)}, u32[]{:S(2)}) async-start(bf16[8,1024,256]{2,1,0:T(8,128)(2,1)} %stack.2), calls=%async_computation | async-start | bytes 8388608 | tf_op jit(solution)/shard_map/all_to_all | solution.py:16
  17.3 0.0 reduce-scatter.2.cloned.1.call-start
  17.3 0.7 reduce
  18.0 0.7 fusion.3
  18.7 0.7 convert_reduce_fusion
  19.4 46.8 %all-to-all-done = bf16[8,1024,256]{2,1,0:T(8,128)(2,1)} async-done(((bf16[8,1024,256]{2,1,0:T(8,128)(2,1)}), bf16[8,1024,256]{2,1,0:T(8,128)(2,1)}, u32[]{:S(2)}, u32[]{:S(2)}) %all-to-all-start) | async-done | bytes 4194336 | tf_op jit(solution)/shard_map/all_to_all | solution.py:16
  66.2 15.1 %gather_fusion = bf16[384,128,256]{2,1,0:T(8,128)(2,1)} fusion(bf16[64,128,256]{2,1,0:T(8,128)(2,1)} %bitcast, s32[1024]{0:T(1024)S(1)} %pad_clamp_fusion), kind=kCustom, calls=%fused_computation | custom fusion | bytes 50333184 | tf_op jit(solution)/shard_map/gather | solution.py:20
  81.3 31.7 %multiply_bitcast_fusion = f32[384,128,256]{1,2,0:T(8,128)} fusion(f32[384]{0:T(512)S(1)} %convert_reduce_fusion, bf16[384,128,256]{2,1,0:T(8,128)(2,1)} %gather_fusion, bf16[1,1,384,128,128]{4,3,2,1,0:T(8,128)(2,1)} %param.10), kind=kOutput, calls=%fused_computation.2 | convolution fusion | flops 3233808384 | bytes 88081920 | tf_op jit(solution)/shard_map/kij,kif->kjf/dot_general | solution.py:21
  113.1 48.8 %copy.12 = f32[384,128,256]{2,1,0:T(8,128)} copy(f32[384,128,256]{1,2,0:T(8,128)} %multiply_bitcast_fusion) | data formatting | bytes 100663296 | tf_op jit(solution)/shard_map/mul | solution.py:22
  161.9 7.8 %broadcast_in_dim.2 = f32[128,128,256]{2,1,0:T(8,128)} broadcast(f32[]{:T(128)} %constant.0.clone.1), dimensions={} | broadcast | bytes 16777220 | tf_op jit(solution)/shard_map/broadcast_in_dim | solution.py:23
  169.7 114.9 %scatter_fusion = f32[128,128,256]{2,1,0:T(8,128)} fusion(f32[128,128,256]{2,1,0:T(8,128)} %broadcast_in_dim.2, s32[384]{0:T(512)S(1)} %reduce, f32[384,128,256]{2,1,0:T(8,128)} %copy.12), kind=kCustom, calls=%fused_computation.1 | custom fusion | flops 12582912 | bytes 150996480 | tf_op jit(solution)/shard_map/scatter-add | solution.py:23
  284.5 0.0 reduce-scatter.2.cloned.1.call-update
  284.6 0.0 all-reduce.2.cloned.1.call-start
  284.6 110.3 %reduce-scatter.2.cloned.1.call-done = f32[1024,256]{1,0:T(8,128)} async-done(((f32[16384,256]{1,0:T(8,128)}), f32[1024,256]{1,0:T(8,128)}) %reduce-scatter.2.cloned.1.call-update) | async-done | bytes 1048592 | tf_op jit(solution)/shard_map/reduce_scatter | solution.py:25
  394.9 0.0 copy-done
  394.9 2.3 convolution_bitcast_fusion
  397.2 0.0 all-reduce.2.cloned.1.call-update
  397.2 0.0 copy-done.1
  397.2 2.4 convolution_convert_fusion
  399.6 142.3 %all-reduce.2.cloned.1.call-done = f32[256,256]{0,1:T(8,128)} async-done(((f32[256,256]{0,1:T(8,128)}), f32[256,256]{0,1:T(8,128)}) %all-reduce.2.cloned.1.call-update) | async-done | bytes 262160 | tf_op jit(solution)/shard_map/psum | solution.py:33
  541.9 1.0 broadcast_multiply_fusion
  542.8 0.8 copy.13
  (2 shorter events, 0.0 us)
Async XLA Ops:
  7.2 387.7 %copy-start = (bf16[1024,256]{1,0:T(8,128)(2,1)S(1)}, bf16[1024,256]{1,0:T(8,128)(2,1)}, u32[]{:S(2)}) copy-start(bf16[1024,256]{1,0:T(8,128)(2,1)} %param.8) | copy-start | bytes 1572868
  10.5 55.7 %all-to-all-start = ((bf16[8,1024,256]{2,1,0:T(8,128)(2,1)}), bf16[8,1024,256]{2,1,0:T(8,128)(2,1)}, u32[]{:S(2)}, u32[]{:S(2)}) async-start(bf16[8,1024,256]{2,1,0:T(8,128)(2,1)} %stack.2), calls=%async_computation | async-start | bytes 8388608 | tf_op jit(solution)/shard_map/all_to_all | solution.py:16
  17.3 377.6 %reduce-scatter.2.cloned.1.call-start = ((), (), s32[]{:S(2)}) async-start(), calls=%async_computation.2 | async-start | bytes 17825792 | tf_op jit(solution)/shard_map/reduce_scatter | solution.py:25
  169.7 227.5 %copy-start.1 = (bf16[256,256]{1,0:T(8,128)(2,1)S(1)}, bf16[256,256]{1,0:T(8,128)(2,1)}, u32[]{:S(2)}) copy-start(bf16[256,256]{1,0:T(8,128)(2,1)} %param.9) | copy-start | bytes 393220
  284.6 257.3 %all-reduce.2.cloned.1.call-start = ((), (), s32[]{:S(2)}) async-start(), calls=%async_computation.3 | async-start | bytes 524288 | tf_op jit(solution)/shard_map/psum | solution.py:33
Sparse Core Ops, SparseCore 0:
  284.7 110.1 reduce-scatter.1
  400.2 141.6 all-reduce.1
